TPU v7x, 128 devices: a whole 4x4x4 slice. The times are simulated.
128 devices in a mesh: pool: 4 (over y), tp: 32 (over x, z, core).
Axes of the slice: x: 4, y: 4, z: 4, core: 2. Of those that a mesh axis runs over, the one named last changes fastest.
Arguments:
- tokens: bfloat16 [2048, 8192], P('pool', 'tp'), may hold values from -6 to 6
- w_query: bfloat16 [8192, 8192], P(None, 'tp'), may hold values from -0.0625 to 0.0625
- w_key: bfloat16 [8192, 8192], P(None, 'tp'), may hold values from -0.0625 to 0.0625
- w_value: bfloat16 [8192, 8192], P(None, 'tp'), may hold values from -0.0625 to 0.0625
- w_gate: bfloat16 [8192, 8192], P(None, 'tp'), may hold values from -0.0625 to 0.0625
- decay: float32 [32], P('tp'), as said below
- pool_states: float32 [32, 32, 256, 256], P('pool', 'tp'), may hold values from -0.75 to 0.75
- lengths: int32 [32], replicated, may hold values from 1 to 128, as said below
- slot_of: int32 [32], replicated, may hold values from 0 to 31, as said below
- serve: int32 [32], replicated, may hold values from 0 to 3, as said below
Outputs:
- retained: bfloat16 [2048, 8192], P('pool', 'tp')
- new_states: float32 [32, 32, 256, 256], P('pool', 'tp')
Inputs may be any that keep to these rules, and one draw needn't show every extreme that they name: `lengths`: each turn has 1 to 128 tokens and some turn exactly 128. The turns served by one group total at most 512 tokens; one group serves exactly 16 sessions whose turns total exactly 512. A permutation of the pool rows; the owner group of session s is slot_of[s] // 8. At most 4 sessions of one owner group are served by one group, and exactly 4 for some pairs of groups. `serve`: A group's turns are packed in increasing session order from the first row of its block of 512 rows; the remaining rows are padding. `decay`: between 0 and 1 for every head.
All inputs are finite; a program needn't handle non-finite values.
Results may differ from a plain program's by a relative error of at most 0.014.
Values may be sent and summed in bfloat16 or wider, within the bound.
A program may use at most 128 MiB of HBM per device.

v0:
```python
import jax
import jax.numpy as jnp
from jax import lax
from jax.sharding import PartitionSpec as P

HEAD = 256
LMAX = 128


norm_epsilon = 1e-05


def on_device(tokens, w_query, w_key, w_value, w_gate, decay, pool_states, lengths, slot_of, serve):
    groups = lax.axis_size("pool")
    this_group = lax.axis_index("pool")
    sessions = lengths.shape[0]
    owned = pool_states.shape[0]
    per_owner = sessions // (2 * groups)
    slot_count = groups * per_owner
    row_count = tokens.shape[0]
    local_heads = decay.shape[0]
    head_width = pool_states.shape[2]
    value_width = pool_states.shape[3]
    turn_most = LMAX
    session_ids = jnp.arange(sessions, dtype=jnp.int32)
    owner_group = slot_of // owned
    same_pair = (owner_group[:, None] == owner_group[None, :]) & (serve[:, None] == serve[None, :])
    order_rank = jnp.sum(
        (same_pair & (slot_of[None, :] < slot_of[:, None])).astype(jnp.int32), axis=1
    )
    same_group = serve[:, None] == serve[None, :]
    turn_start = jnp.sum(
        jnp.where(same_group & (session_ids[None, :] < session_ids[:, None]), lengths[None, :], 0),
        axis=1,
    )
    served_here = serve == this_group
    recv_slot = owner_group * per_owner + order_rank
    places = jnp.arange(slot_count, dtype=jnp.int32)
    slot_match = (served_here[None, :] & (recv_slot[None, :] == places[:, None])).astype(jnp.int32)
    slot_len = jnp.sum(slot_match * lengths[None, :], axis=1)
    slot_start = jnp.sum(slot_match * turn_start[None, :], axis=1)
    pooled = lax.all_gather(pool_states.astype(jnp.bfloat16), "pool", axis=0, tiled=True).astype(
        pool_states.dtype
    )
    pool_index = jnp.sum(slot_match * slot_of[None, :], axis=1)
    initial = jnp.take(pooled, pool_index, axis=0)
    weights = (w_query, w_key, w_value, w_gate)
    tile_cols = lax.all_gather(tokens, "tp", axis=1, tiled=True)
    query, keys, values, gate = tuple(
        (jnp.dot(tile_cols, matrix, preferred_element_type=jnp.float32) for matrix in weights)
    )
    query = query.astype(jnp.bfloat16).reshape(row_count, local_heads, head_width)
    keys = (keys * HEAD ** (-0.5)).astype(jnp.bfloat16).reshape(row_count, local_heads, head_width)
    values = values.astype(jnp.bfloat16).reshape(row_count, local_heads, value_width)
    gate = gate.astype(jnp.bfloat16)
    row_index = jnp.arange(row_count, dtype=jnp.int32)
    inside = (
        served_here[None, :]
        & (row_index[:, None] >= turn_start[None, :])
        & (row_index[:, None] < (turn_start + lengths)[None, :])
    ).astype(jnp.int32)
    is_live = jnp.sum(inside, axis=1) > 0
    turn_id = jnp.where(is_live, jnp.sum(inside * session_ids[None, :], axis=1), -1)
    position = row_index - jnp.sum(inside * turn_start[None, :], axis=1)
    log_gamma = jnp.log(decay)
    same_turn = (
        (turn_id[:, None] == turn_id[None, :])
        & (turn_id[:, None] >= 0)
        & (row_index[None, :] <= row_index[:, None])
    )
    distance = (position[:, None] - position[None, :]).astype(jnp.float32)
    scores = jnp.einsum("thd,jhd->htj", query, keys, preferred_element_type=jnp.float32)
    weight = jnp.where(
        same_turn[None], jnp.exp(jnp.maximum(distance, 0.0)[None] * log_gamma[:, None, None]), 0.0
    )
    mixing = (scores * weight).astype(jnp.bfloat16)
    inside_sum = jnp.einsum("htj,jhd->thd", mixing, values, preferred_element_type=jnp.float32)
    query_pad = jnp.concatenate(
        [query, jnp.zeros((turn_most, local_heads, head_width), jnp.bfloat16)], axis=0
    )
    key_pad = jnp.concatenate(
        [keys, jnp.zeros((turn_most, local_heads, head_width), jnp.bfloat16)], axis=0
    )
    value_pad = jnp.concatenate(
        [values, jnp.zeros((turn_most, local_heads, value_width), jnp.bfloat16)], axis=0
    )
    offsets = jnp.arange(turn_most, dtype=jnp.int32)

    def visit_slot(slot_num, carry):
        carried, updated = carry
        first_row = slot_start[slot_num]
        turn_len = slot_len[slot_num]
        query_rows = lax.dynamic_slice_in_dim(query_pad, first_row, turn_most, 0).astype(
            jnp.float32
        )
        key_rows = lax.dynamic_slice_in_dim(key_pad, first_row, turn_most, 0).astype(jnp.float32)
        value_rows = lax.dynamic_slice_in_dim(value_pad, first_row, turn_most, 0).astype(
            jnp.float32
        )
        prior_state = lax.dynamic_index_in_dim(initial, slot_num, 0, keepdims=False)
        in_turn = offsets < turn_len
        reach_decay = jnp.where(
            in_turn[:, None],
            jnp.exp((offsets[:, None] + 1).astype(jnp.float32) * log_gamma[None, :]),
            0.0,
        )
        carry_term = (
            jnp.einsum("rhd,hde->rhe", query_rows, prior_state, precision=lax.Precision.HIGHEST)
            * reach_decay[:, :, None]
        )
        existing = lax.dynamic_slice_in_dim(carried, first_row, turn_most, 0)
        carried = lax.dynamic_update_slice_in_dim(carried, existing + carry_term, first_row, 0)
        tail_decay = jnp.where(
            in_turn[:, None],
            jnp.exp((turn_len - 1 - offsets)[:, None].astype(jnp.float32) * log_gamma[None, :]),
            0.0,
        )
        next_state = jnp.exp(turn_len.astype(jnp.float32) * log_gamma)[
            :, None, None
        ] * prior_state + jnp.einsum(
            "rhd,rhe->hde",
            key_rows * tail_decay[:, :, None],
            value_rows,
            precision=lax.Precision.HIGHEST,
        )
        updated = lax.dynamic_update_index_in_dim(updated, next_state, slot_num, 0)
        return (carried, updated)

    carried, updated = lax.fori_loop(
        0,
        slot_count,
        visit_slot,
        (
            jnp.zeros((row_count + turn_most, local_heads, value_width), jnp.float32),
            jnp.zeros_like(initial),
        ),
    )
    mixed = inside_sum + carried[:row_count]
    row_mean = jnp.mean(mixed, axis=-1, keepdims=True)
    centered = mixed - row_mean
    variance = jnp.mean(centered * centered, axis=-1, keepdims=True)
    normed = centered * lax.rsqrt(variance + norm_epsilon)
    gated = (
        jax.nn.silu(gate.astype(jnp.float32)).reshape(row_count, local_heads, value_width) * normed
    )
    retained = (
        (gated * is_live[:, None, None].astype(jnp.float32))
        .astype(jnp.bfloat16)
        .reshape(row_count, local_heads * value_width)
    )
    outgoing_back = updated.reshape(groups, per_owner, local_heads, head_width, value_width)
    returned = (
        lax.all_to_all(
            outgoing_back.astype(jnp.bfloat16), "pool", split_axis=0, concat_axis=0, tiled=True
        )
        .astype(outgoing_back.dtype)
        .reshape(slot_count, local_heads, head_width, value_width)
    )
    local_rows = jnp.arange(owned, dtype=jnp.int32) + this_group * owned
    which_row = (slot_of[None, :] == local_rows[:, None]).astype(jnp.int32)
    back_index = jnp.sum(which_row * (serve * per_owner + order_rank)[None, :], axis=1)
    new_pool = jnp.take(returned, back_index, axis=0)
    return (retained, new_pool)


def solution(mesh):
    return jax.shard_map(
        on_device,
        mesh=mesh,
        in_specs=(
            P("pool", "tp"),
            P(None, "tp"),
            P(None, "tp"),
            P(None, "tp"),
            P(None, "tp"),
            P("tp"),
            P("pool", "tp", None, None),
            P(),
            P(),
            P(),
        ),
        out_specs=(P("pool", "tp"), P("pool", "tp", None, None)),
        check_vma=False,
    )
```

profile of v0, /device:TPU:1, one launch (start us, length us, event | category | flops | bytes accessed | tf_op | source)
XLA Modules:
  0.0 337.5 jit_solution(12733766502636768944)
XLA Ops:
  7.2 2.8 convert_element_type.129
  13.4 48.3 %all-gather.5.cloned.1.call-done = bf16[32,1,256,256]{3,2,1,0:T(8,128)(2,1)} async-done(((bf16[8,1,256,256]{3,2,1,0:T(8,128)(2,1)}), bf16[32,1,256,256]{3,2,1,0:T(8,128)(2,1)}) %all-gather.5.cloned.1.call-update) | async-done | bytes 4194320 | tf_op jit(solution)/shard_map/all_gather | solution.py:42
  61.7 6.5 %bitcast_convert_fusion = f32[32,256,256]{2,1,0:T(8,128)} fusion(bf16[32,1,256,256]{3,2,1,0:T(8,128)(2,1)} %all-gather.5.cloned.1.call-done), kind=kLoop, calls=%fused_computation.35 | loop fusion | flops 2097152 | bytes 12582912 | tf_op jit(solution)/shard_map/convert_element_type | solution.py:42
  68.1 6.1 %gather_fusion = f32[16,256,256]{2,1,0:T(8,128)} fusion(f32[32,256,256]{2,1,0:T(8,128)} %bitcast_convert_fusion, s32[1024]{0:T(1024)S(1)} %pad_clamp_fusion.1), kind=kCustom, calls=%fused_computation | custom fusion | bytes 8388672 | tf_op jit(solution)/shard_map/jit(_take)/gather | solution.py:46
  74.3 4.7 %fusion.24 = f32[16,1,256,256]{3,2,1,0:T(8,128)} fusion(f32[16,256,256]{2,1,0:T(8,128)} %gather_fusion, pred[16]{0:T(512)(128)(4,1)S(1)} %compare_and_fusion.3), kind=kLoop, calls=%fused_computation.37 | loop fusion | flops 1048576 | bytes 8388624
  78.9 45.4 %all-gather.3.cloned.1.call-done = bf16[512,8192]{1,0:T(8,128)(2,1)} async-done(((bf16[512,256]{1,0:T(8,128)(2,1)}), bf16[512,8192]{1,0:T(8,128)(2,1)}) %all-gather.3.cloned.1.call-update) | async-done | bytes 8388624 | tf_op jit(solution)/shard_map/all_gather | solution.py:48
  124.3 7.0 %fusion.27 = bf16[512,256]{1,0:T(8,128)(2,1)S(1)} fusion(bf16[512,8192]{1,0:T(8,128)(2,1)} %all-gather.3.cloned.1.call-done, bf16[8192,256]{1,0:T(8,128)(2,1)} %param.14), kind=kOutput, calls=%fused_computation.45 | convolution fusion | flops 2147745792 | bytes 12845056 | tf_op jit(solution)/shard_map/dot_general | solution.py:50
  132.5 2.3 convolution_convert_fusion.1
  134.9 2.3 convolution_convert_fusion
  137.9 156.2 %while.19 = (s32[]{:T(128)}, f32[640,1,256]{2,0,1:T(8,128)S(1)}, bf16[16,1,256,256]{3,2,1,0:T(8,128)(2,1)}, s32[16]{0:T(128)S(1)}, f32[16,1,256,256]{3,2,1,0:T(8...) while((s32[]{:T(128)}, f32[640,1,256]{2,0,1:T(8,128)S(1)}, ...), condition=%wide.region_9.10_spmd.clone.clone, body=%wide.region_8.9_spmd.clone.clone.sunk | while | flops 201589888 | bytes 2690823 | solution.py:129
  143.1 1.9 fusion.82
  152.9 1.9 fusion.82
  162.7 1.9 fusion.82
  172.4 1.9 fusion.82
  182.2 1.9 fusion.82
  192.0 1.9 fusion.82
  201.7 1.9 fusion.82
  211.5 1.9 fusion.82
  221.2 1.9 fusion.82
  231.0 1.9 fusion.82
  240.8 1.9 fusion.82
  250.5 1.9 fusion.82
  260.3 1.9 fusion.82
  270.0 1.9 fusion.82
  279.8 1.9 fusion.82
  289.5 1.9 fusion.82
  294.1 3.8 %all-to-all-start = ((bf16[4,4,1,256,256]{4,3,1,2,0:T(8,128)(2,1)}), bf16[4,4,1,256,256]{4,3,1,2,0:T(8,128)(2,1)S(1)}, u32[]{:S(2)}, u32[]{:S(2)}) async-start(bf16[4,4,1,256,256]{4,3,1,2,0:T(8,128)(2,1)} %bitcast.116), calls=%async_computation | async-start | bytes 4194304 | tf_op jit(solution)/shard_map/all_to_all | solution.py:153
  297.9 2.3 fusion.57
  301.1 7.7 %fusion.46 = bf16[512,256]{1,0:T(8,128)(2,1)} fusion(bf16[512,8192]{1,0:T(8,128)(2,1)} %all-gather.3.cloned.1.call-done, bf16[8192,256]{1,0:T(8,128)(2,1)} %param.16, f32[512,1,256]{2,0,1:T(8,128)S(1)} %get-tuple-element.401, f32[512]{0:T(512)S(1)} %get-tuple-element.392, f32[512]{0:T(512)S(1)} %add_rsqrt_fusion, f32[512]{0:T(512)S(1)} %broadcast_multiply_fusion), kind=kOutput, calls=%fused_computation.69 | convolution fusion | flops 2148925440 | bytes 13375488 | tf_op jit(solution)/shard_map/dot_general | solution.py:50
  308.8 14.9 %all-to-all-done = bf16[4,4,1,256,256]{4,3,1,2,0:T(8,128)(2,1)S(1)} async-done(((bf16[4,4,1,256,256]{4,3,1,2,0:T(8,128)(2,1)}), bf16[4,4,1,256,256]{4,3,1,2,0:T(8,128)(2,1)S(1)}, u32[]{:S(2)}, u32[]{:S(2)}) %all-to-all-start) | async-done | bytes 2097184 | tf_op jit(solution)/shard_map/all_to_all | solution.py:153
  323.7 2.5 bitcast_convert_fusion.1
  326.2 2.9 gather_fusion.1
  (209 shorter events, 80.5 us)
Async XLA Ops:
  7.2 4.3 %copy-start.2 = (s32[32]{0:T(128)S(1)}, s32[32]{0:T(128)}, u32[]{:S(2)}) copy-start(s32[32]{0:T(128)} %param.20) | copy-start | bytes 388
  7.2 4.4 %copy-start.4 = (s32[32]{0:T(128)S(1)}, s32[32]{0:T(128)}, u32[]{:S(2)}) copy-start(s32[32]{0:T(128)} %param.19) | copy-start | bytes 388
  7.2 4.4 %copy-start.3 = (s32[32]{0:T(128)S(1)}, s32[32]{0:T(128)}, u32[]{:S(2)}) copy-start(s32[32]{0:T(128)} %param.21) | copy-start | bytes 388
  7.2 54.5 %all-gather.5.cloned.1.call-start = ((), (), s32[]{:S(2)}) async-start(), calls=%async_computation.2 | async-start | bytes 5242880 | tf_op jit(solution)/shard_map/all_gather | solution.py:42
  10.0 114.3 %all-gather.3.cloned.1.call-start = ((), (), s32[]{:S(2)}) async-start(), calls=%async_computation.1 | async-start | bytes 8650752 | tf_op jit(solution)/shard_map/all_gather | solution.py:48
  124.3 7.1 %copy-start.6 = (bf16[512,8192]{1,0:T(8,128)(2,1)S(1)}, bf16[512,8192]{1,0:T(8,128)(2,1)}, u32[]{:S(2)}) copy-start(bf16[512,8192]{1,0:T(8,128)(2,1)} %all-gather.3.cloned.1.call-done) | copy-start | bytes 25165828
  124.3 8.2 %copy-start.7 = (bf16[8192,256]{1,0:T(8,128)(2,1)S(1)}, bf16[8192,256]{1,0:T(8,128)(2,1)}, u32[]{:S(2)}) copy-start(bf16[8192,256]{1,0:T(8,128)(2,1)} %param.15) | copy-start | bytes 12582916
  132.5 2.4 copy-start.8
  134.8 2.4 copy-start
  137.2 0.7 copy-start.1
  294.1 29.6 %all-to-all-start = ((bf16[4,4,1,256,256]{4,3,1,2,0:T(8,128)(2,1)}), bf16[4,4,1,256,256]{4,3,1,2,0:T(8,128)(2,1)S(1)}, u32[]{:S(2)}, u32[]{:S(2)}) async-start(bf16[4,4,1,256,256]{4,3,1,2,0:T(8,128)(2,1)} %bitcast.116), calls=%async_computation | async-start | bytes 4194304 | tf_op jit(solution)/shard_map/all_to_all | solution.py:153
  308.8 20.3 %copy-start.5 = (pred[8]{0:T(512)(128)(4,1)S(1)}, pred[8]{0:T(512)(128)(4,1)}, u32[]{:S(2)}) copy-start(pred[8]{0:T(512)(128)(4,1)} %compare_and_fusion.2) | copy-start | bytes 28
Sparse Core Ops, SparseCore 0:
  10.2 51.4 all-gather.4
  63.9 60.3 all-gather.2
where the time goes:
time: 340 us; the launch traced here: 338 us
  waiting for transfers between devices  109 us (32%)
  matrix products  74.1 us (22%)
  loops' own time  51.6 us (15%)
  local copies, waits for them, and re-layouts  49.6 us (15%)
  other arithmetic  34 us (10%)
  between operations  15 us (4%)
  starting transfers between devices  3.88 us (1%)
    another operation x1, loops' own time, on_device(): lax.fori_loop(0, slot_count, visit_slot, (jnp.zeros((row_count + turn_mos...  51.6 us
    all_gather x1, waiting for transfers between devices, on_device(): lax.all_gather(pool_states.astype(jnp.bfloat16), 'pool', axis=0, tiled=True)  48.3 us
    all_gather x1, waiting for transfers between devices, on_device(): tile_cols = lax.all_gather(tokens, 'tp', axis=1, tiled=True)  45.4 us
    dot_general x16, matrix products, visit_slot(): jnp.einsum('rhd,rhe->hde', key_rows * tail_decay[:, :, None], value_rows,...  31 us
    dot_general x16, matrix products, visit_slot(): jnp.einsum('rhd,hde->rhe', query_rows, prior_state, precision=lax.Precisi...  21.5 us
    dot_general x4, matrix products, on_device(): jnp.dot(tile_cols, matrix, preferred_element_type=jnp.float32)  19.4 us
    dynamic_update_slice x32, local copies, waits for them, and re-layouts, visit_slot(): lax.dynamic_update_slice_in_dim(carried, existing + carry_term, first_row...  17.4 us
    all_to_all x1, waiting for transfers between devices, on_device(): lax.all_to_all(outgoing_back.astype(jnp.bfloat16), 'pool', split_axis=0,...  14.9 us
  transfers between devices with their start and end apart: 3, of which 3 were waited for; matrix products, arithmetic and copies ran while one was open for 9% of the time, Pallas kernels for 0%

commit v1 on v0

v1 whole, which is shorter than its diff:
```python
import functools

import jax
import jax.numpy as jnp
from jax import lax
from jax.experimental import pallas as pl
from jax.experimental.pallas import tpu as pltpu
from jax.sharding import PartitionSpec as P

MESH = pl.DeviceIdType.MESH
HEAD = 256
ROWS = 512
SESSIONS = 32
OWNED = 8
SLOTS = 4
CHUNKS = 2
CHUNK = ROWS // CHUNKS
PER = CHUNK // 128
EPSILON = 1e-05
F32 = jnp.float32
BF16 = jnp.bfloat16


def kernel(
    tokens, w_query, w_key, w_value, w_gate, pool, decay, lengths, slot_of, serve,
    retained, keyval_out, *scratch,
):
    lines = [scratch[4 * r:4 * r + 4] for r in range(CHUNKS)]
    scratch = scratch[4 * CHUNKS:]
    twins = [scratch[4 * r:4 * r + 4] for r in range(CHUNKS)]
    scratch = scratch[4 * CHUNKS:]
    prior, packed, keyval, scratch = scratch[:4], scratch[4:7], scratch[7:11], scratch[11:]
    (
        weights, prior_own, query, gate, total, starts,
        token_sem, pool_sem, weight_sem, out_sem,
        near_send, near_recv, far_send, far_recv, twin_send, twin_recv,
        state_send, state_recv, kv_send, kv_recv, relay_send, relay_recv,
    ) = scratch
    me = lax.axis_index("pool")
    place = lax.axis_index("tp")
    x, z, core = place // 8, (place // 2) % 4, place % 2
    u = x * (1 - core) + z * core
    v = z * (1 - core) + x * core

    def at(u_at, v_at):
        u_at, v_at = (u_at + 4) % 4, (v_at + 4) % 4
        x_at = u_at * (1 - core) + v_at * core
        z_at = v_at * (1 - core) + u_at * core
        return {"tp": x_at * 8 + z_at * 2 + core}

    twin = {"tp": x * 8 + z * 2 + (1 - core)}

    def group(offset):
        return {"pool": (me + offset + 4) % 4}

    def remote(src, dst, send, recv, device):
        return pltpu.make_async_remote_copy(
            src_ref=src, dst_ref=dst, send_sem=send, recv_sem=recv,
            device_id=device, device_id_type=MESH,
        )

    def rows_of(r):
        return pl.ds(pl.multiple_of(r * CHUNK, CHUNK), CHUNK)

    token_copies = [
        pltpu.make_async_copy(
            tokens.at[pl.ds(r * CHUNK, CHUNK)], lines[r][0].at[0], token_sem.at[r]
        )
        for r in range(CHUNKS)
    ]
    for copy in token_copies:
        copy.start()
    pool_copy = pltpu.make_async_copy(pool, prior_own, pool_sem)
    pool_copy.start()
    matrices = (w_query, w_key, w_value, w_gate)

    def weight_copy(plane, line, which):
        source = matrices[which]
        part = source.at[:, line, 0] if plane == 0 else source.at[line, :, 1]
        return pltpu.make_async_copy(
            part, weights.at[plane, line, which], weight_sem.at[plane, line, which]
        )

    for line in range(4):
        for plane in range(2):
            for which in range(4):
                weight_copy(plane, line, which).start()

    partners = [at(u + d, v) for d in (1, 2, 3)] + [at(u, v + d) for d in (1, 2, 3)]
    partners += [twin] + [group(d) for d in (1, 2, 3)]
    barrier = pltpu.get_barrier_semaphore()
    for partner in partners:
        pl.semaphore_signal(barrier, inc=1, device_id=partner, device_id_type=MESH)
    pl.semaphore_wait(barrier, len(partners))

    def near(r, d):
        return remote(
            lines[r][0].at[0], lines[r][0].at[d],
            near_send.at[r, d - 1], near_recv.at[r, d - 1], at(u + d, v),
        )

    def far(r, d):
        return remote(
            lines[r][0], lines[r][d], far_send.at[r, d - 1], far_recv.at[r, d - 1], at(u, v + d)
        )

    def to_twin(r, d):
        return remote(lines[r][d], twins[r][d], twin_send.at[r, d], twin_recv.at[r, d], twin)

    for r in range(CHUNKS):
        token_copies[r].wait()
        for d in (1, 3, 2):
            near(r, d).start()

    zero = jnp.int32(0)

    def scan(s, carry):
        own_rows, own_count, ids, id_count, run = carry
        slot, to, long = slot_of[s], serve[s], lengths[s]
        owner, row = slot // OWNED, slot % OWNED
        begin = zero
        new_run = []
        for g in range(4):
            begin = jnp.where(to == g, run[g], begin)
            new_run.append(run[g] + jnp.where(to == g, long, 0))
        starts[s] = begin
        mine, here = owner == me, to == me
        ahead, behind = (to - me + 4) % 4, (me - owner + 4) % 4
        own_rows_n, own_count_n, ids_n, id_count_n = [], [], [], []
        for g in range(4):
            hit = mine & (ahead == g)
            own_rows_n.append(jnp.where(hit, own_rows[g] * 8 + row, own_rows[g]))
            own_count_n.append(own_count[g] + jnp.where(hit, 1, 0))
            hit = here & (behind == g)
            ids_n.append(jnp.where(hit, ids[g] * 32 + s, ids[g]))
            id_count_n.append(id_count[g] + jnp.where(hit, 1, 0))
        return (
            tuple(own_rows_n), tuple(own_count_n), tuple(ids_n), tuple(id_count_n),
            tuple(new_run),
        )

    four = (zero,) * 4
    own_rows, _, ids, id_count, _ = lax.fori_loop(
        0, SESSIONS, scan, (four, four, four, four, four)
    )

    def state(d, k):
        return remote(
            packed[d - 1].at[k], prior[d].at[k],
            state_send.at[d - 1, k], state_recv.at[d - 1, k], group(d),
        )

    pool_copy.wait()
    for k in range(SLOTS):
        for d in (2, 1, 3):
            packed[d - 1][k] = prior_own[(own_rows[d] >> (3 * k)) & 7].astype(BF16)
            state(d, k).start()
    for k in range(SLOTS):
        prior[0][k] = prior_own[(own_rows[0] >> (3 * k)) & 7].astype(BF16)

    def send_far(r):
        for d in (1, 2, 3):
            near(r, d).wait_recv()
        for d in (1, 3, 2):
            far(r, d).start()

    def multiply(part, plane, line, first):
        left = jnp.concatenate([part[i] for i in range(4)], axis=1)

        def one(which, _):
            right = jnp.concatenate(
                [weights[plane, line, which, (first - i + 4) % 4] for i in range(4)], axis=0
            )
            total[which] += jnp.dot(left, right, preferred_element_type=F32)
            return 0

        lax.fori_loop(0, 4, one, 0)

    def side(way):
        return group(1 if way == 0 else -1)

    def kv_out(r, way):
        return remote(
            keyval[0].at[r], keyval[1 + way].at[r], kv_send.at[r, way], kv_recv.at[r, way], side(way)
        )

    def relay(r, way):
        return remote(
            keyval[1 + way].at[r, way], keyval[3].at[r, way],
            relay_send.at[r, way], relay_recv.at[r, way], side(way),
        )

    send_far(0)
    for line in range(4):
        for plane in range(2):
            for which in range(4):
                weight_copy(plane, line, which).wait()

    for r in range(CHUNKS):
        total[...] = jnp.zeros_like(total)
        for j, d in enumerate((0, 1, 3, 2)):
            if j > 0:
                far(r, d).wait_recv()
            to_twin(r, d).start()
            if j == 2 and r + 1 < CHUNKS:
                send_far(r + 1)
            multiply(lines[r][d], core, (v - d + 4) % 4, u)
            to_twin(r, d).wait_recv()
            multiply(twins[r][d], 1 - core, (u - d + 4) % 4, v)
        query[r * CHUNK:(r + 1) * CHUNK, :] = total[0].astype(BF16)
        keyval[0][r, 0] = (total[1] * HEAD ** (-0.5)).astype(BF16)
        keyval[0][r, 1] = total[2].astype(BF16)
        gate[r * CHUNK:(r + 1) * CHUNK, :] = total[3].astype(BF16)
        kv_out(r, 0).start()
        kv_out(r, 1).start()

    def pass_on(r):
        for way in range(2):
            kv_out(r, way).wait_recv()
            relay(r, way).start()

    pass_on(0)

    for k in range(SLOTS):
        for d in (1, 2, 3):
            state(d, k).wait_recv()

    log_gamma = jnp.log(jnp.full((1, 1), decay[0], F32))

    first, last = [], []
    for g in range(4):
        for k in range(SLOTS):
            s = (ids[g] >> (5 * k)) & 31
            first.append(starts[s])
            last.append(jnp.where(k < id_count[g], starts[s] + lengths[s], 0))

    def own_rows_of(which):
        return jnp.concatenate([keyval[0][n, which] for n in range(CHUNKS)], axis=0)

    def retain(r, _):
        row = lax.broadcasted_iota(jnp.int32, (CHUNK, 1), 0) + r * CHUNK
        live = jnp.zeros((CHUNK, 1), jnp.bool_)
        begin = jnp.full((CHUNK, 1), ROWS, jnp.int32)
        q = query[rows_of(r), :]
        carried = jnp.zeros((CHUNK, HEAD), F32)
        for g in range(4):
            parts = []
            for k in range(SLOTS):
                n = g * SLOTS + k
                inside = (row >= first[n]) & (row < last[n])
                begin = jnp.where(inside, first[n], begin)
                parts.append(jnp.where(inside, q, jnp.zeros_like(q)))
            carried += jnp.dot(
                jnp.concatenate(parts, axis=1), prior[g][...].reshape(SLOTS * HEAD, HEAD),
                preferred_element_type=F32,
            )
        live = begin < ROWS
        column = lax.broadcasted_iota(jnp.int32, (CHUNK, ROWS), 1)
        distance = row - column
        scores = lax.dot_general(
            q, own_rows_of(0), (((1,), (1,)), ((), ())), preferred_element_type=F32
        )
        weight = jnp.exp(jnp.maximum(distance, 0).astype(F32) * log_gamma)
        mixing = jnp.where((distance >= 0) & (column >= begin), scores * weight, 0.0).astype(BF16)
        mixed = jnp.dot(
            mixing, own_rows_of(1), preferred_element_type=F32
        )
        reach = jnp.exp(jnp.maximum(row - begin + 1, 0).astype(F32) * log_gamma)
        mixed = mixed + carried * jnp.where(live, reach, 0.0)
        centered = mixed - jnp.mean(mixed, axis=-1, keepdims=True)
        variance = jnp.mean(centered * centered, axis=-1, keepdims=True)
        normed = centered * lax.rsqrt(variance + EPSILON)
        out = gate[rows_of(r), :].astype(F32)
        out = out * (1.0 / (1.0 + jnp.exp(-out))) * normed
        retained[rows_of(r), :] = jnp.where(live, out, 0.0).astype(BF16)
        return 0

    lax.fori_loop(0, CHUNKS, retain, 0)
    for r in range(1, CHUNKS):
        pass_on(r)
    for r in range(CHUNKS):
        for way in range(2):
            relay(r, way).wait_recv()
    out_copies = [
        pltpu.make_async_copy(keyval[n], keyval_out.at[n], out_sem.at[n]) for n in range(4)
    ]
    for copy in out_copies:
        copy.start()
    for r in range(CHUNKS):
        for d in (1, 2, 3):
            near(r, d).wait_send()
            far(r, d).wait_send()
        for d in range(4):
            to_twin(r, d).wait_send()
        for way in range(2):
            kv_out(r, way).wait_send()
            relay(r, way).wait_send()
    for k in range(SLOTS):
        for d in (1, 2, 3):
            state(d, k).wait_send()
    for copy in out_copies:
        copy.wait()


def update(keyval, pool, decay, lengths, slot_of, serve, new_states, starts):
    me = lax.axis_index("pool")
    zero = jnp.int32(0)

    def scan(s, run):
        to = serve[s]
        begin = zero
        for g in range(4):
            begin = jnp.where(to == g, run[g], begin)
        slot = slot_of[s]

        @pl.when(slot // OWNED == me)
        def _():
            away = (me - to + 4) % 4
            starts[0, slot % OWNED] = jnp.where(away == 3, 2, jnp.where(away == 2, 3, away))
            starts[1, slot % OWNED] = begin
            starts[2, slot % OWNED] = lengths[s]

        return tuple(run[g] + jnp.where(to == g, lengths[s], 0) for g in range(4))

    lax.fori_loop(0, SESSIONS, scan, (zero,) * 4)
    log_gamma = jnp.log(jnp.full((1, 1), decay[0], F32))

    def one(i, _):
        place, begin, long = starts[0, i], starts[1, i], starts[2, i]
        low = jnp.minimum(begin // 128, ROWS // 128 - 2)
        row = lax.broadcasted_iota(jnp.int32, (256, 1), 0) + low * 128

        def rows_at(which):
            return jnp.concatenate(
                [
                    keyval[
                        place, (low + n) // PER, which,
                        pl.ds(pl.multiple_of((low + n) % PER * 128, 128), 128), :,
                    ]
                    for n in range(2)
                ],
                axis=0,
            )

        behind = begin + long - 1 - row
        tail = jnp.exp(jnp.maximum(behind, 0).astype(F32) * log_gamma)
        tail = jnp.where((row >= begin) & (behind >= 0), tail, 0.0)
        k_rows = rows_at(0).astype(F32) * tail
        v_rows = rows_at(1)
        change = lax.dot_general(
            k_rows.astype(BF16), v_rows, (((0,), (0,)), ((), ())), preferred_element_type=F32
        )
        keep = jnp.exp(jnp.full((1, 1), long, jnp.int32).astype(F32) * log_gamma)
        new_states[i] = keep * pool[i] + change
        return 0

    lax.fori_loop(0, OWNED, one, 0, unroll=2)


def on_device(tokens, w_query, w_key, w_value, w_gate, decay, pool_states, lengths, slot_of, serve):
    hbm = pl.BlockSpec(memory_space=pl.ANY)
    vmem = pl.BlockSpec(memory_space=pltpu.VMEM)
    smem = pl.BlockSpec(memory_space=pltpu.SMEM)
    dma = pltpu.SemaphoreType.DMA
    split = [w.reshape(4, 4, 2, HEAD, HEAD) for w in (w_query, w_key, w_value, w_gate)]
    states = pool_states.reshape(OWNED, HEAD, HEAD)
    retained, keyval = pl.pallas_call(
        kernel,
        out_shape=(
            jax.ShapeDtypeStruct((ROWS, HEAD), BF16),
            jax.ShapeDtypeStruct((4, CHUNKS, 2, CHUNK, HEAD), BF16),
        ),
        in_specs=[hbm] * 6 + [smem] * 4,
        out_specs=(vmem, hbm),
        scratch_shapes=[
            *[pltpu.VMEM((4, CHUNK, HEAD), BF16)] * (8 * CHUNKS),
            *[pltpu.VMEM((SLOTS, HEAD, HEAD), BF16)] * 7,
            *[pltpu.VMEM((CHUNKS, 2, CHUNK, HEAD), BF16)] * 4,
            pltpu.VMEM((2, 4, 4, 4, HEAD, HEAD), BF16),
            pltpu.VMEM((OWNED, HEAD, HEAD), F32),
            pltpu.VMEM((ROWS, HEAD), BF16),
            pltpu.VMEM((ROWS, HEAD), BF16),
            pltpu.VMEM((4, CHUNK, HEAD), F32),
            pltpu.SMEM((SESSIONS,), jnp.int32),
            dma((CHUNKS,)), dma, dma((2, 4, 4)), dma((4,)),
            dma((CHUNKS, 3)), dma((CHUNKS, 3)),
            dma((CHUNKS, 3)), dma((CHUNKS, 3)),
            dma((CHUNKS, 4)), dma((CHUNKS, 4)),
            dma((3, SLOTS)), dma((3, SLOTS)),
            dma((CHUNKS, 2)), dma((CHUNKS, 2)),
            dma((CHUNKS, 2)), dma((CHUNKS, 2)),
        ],
        compiler_params=pltpu.CompilerParams(
            collective_id=0, has_side_effects=True, vmem_limit_bytes=56 << 20
        ),
        cost_estimate=pl.CostEstimate(
            flops=11_000_000_000, bytes_accessed=24_000_000, transcendentals=1_000_000
        ),
    )(tokens, *split, states, decay, lengths, slot_of, serve)
    new_states = pl.pallas_call(
        update,
        out_shape=jax.ShapeDtypeStruct((OWNED, HEAD, HEAD), F32),
        in_specs=[vmem, vmem] + [smem] * 4,
        out_specs=vmem,
        scratch_shapes=[pltpu.SMEM((3, OWNED), jnp.int32)],
        compiler_params=pltpu.CompilerParams(vmem_limit_bytes=24 << 20),
        cost_estimate=pl.CostEstimate(
            flops=300_000_000, bytes_accessed=6_000_000, transcendentals=2048
        ),
    )(keyval, states, decay, lengths, slot_of, serve)
    return retained, new_states.reshape(OWNED, 1, HEAD, HEAD)


def solution(mesh):
    return jax.shard_map(
        on_device,
        mesh=mesh,
        in_specs=(
            P("pool", "tp"),
            P(None, "tp"),
            P(None, "tp"),
            P(None, "tp"),
            P(None, "tp"),
            P("tp"),
            P("pool", "tp", None, None),
            P(),
            P(),
            P(),
        ),
        out_specs=(P("pool", "tp"), P("pool", "tp", None, None)),
        check_vma=False,
    )
```

time: 340 us -> 82 us (0.24)
  waiting for transfers between devices: 109 us -> 0 us
  Pallas kernels: 0 us -> 78.1 us
  matrix products: 74.1 us -> 0 us
  loops' own time: 51.6 us -> 0 us
  local copies, waits for them, and re-layouts: 49.6 us -> 2.31 us
  other arithmetic: 34 us -> 0 us
  between operations: 15 us -> 1.36 us
  starting transfers between devices: 3.88 us -> 0 us
    all_gather x2 -> x0, waiting for transfers between devices: 93.7 us -> none  [the longest x1 48.3 us: on_device(): lax.all_gather(pool_states.astype(jnp.bfloat16), 'pool', axis=0, tiled=True)]
    pallas_call x0 -> x2, Pallas kernels: none -> 78.1 us  [the longest x1 73.8 us: on_device(): pl.pallas_call(kernel, out_shape=(jax.ShapeDtypeStruct((ROWS, HEAD), BF16...]
    dot_general x37 -> x0, matrix products: 74.1 us -> none  [the longest x16 31 us: visit_slot(): jnp.einsum('rhd,rhe->hde', key_rows * tail_decay[:, :, None], value_rows,...]
    another operation x1 -> x0, loops' own time: 51.6 us -> none  [on_device(): lax.fori_loop(0, slot_count, visit_slot, (jnp.zeros((row_count + turn_mos...]
    dynamic_slice x80 -> x0, local copies, waits for them, and re-layouts: 21.4 us -> none  [the longest x16 9.68 us: visit_slot(): turn_len = slot_len[slot_num]]
    dynamic_update_slice x32 -> x0, local copies, waits for them, and re-layouts: 17.4 us -> none  [visit_slot(): lax.dynamic_update_slice_in_dim(carried, existing + carry_term, first_row...]
    all_to_all x1 -> x0, waiting for transfers between devices: 14.9 us -> none  [on_device(): lax.all_to_all(outgoing_back.astype(jnp.bfloat16), 'pool', split_axis=0,...]
    select_n x20 -> x0, other arithmetic: 11.7 us -> none  [the longest x16 10 us: visit_slot(): jnp.where(in_turn[:, None], jnp.exp((turn_len - 1 - offsets)[:, None].ast...]
  transfers between devices with their start and end apart: 3 -> 0, of which waited for: 3 -> 0; matrix products, arithmetic and copies ran while one was open for 9% -> 0% of each run, Pallas kernels for 0% -> 0%
where the time goes in v1:
time: 82 us; the launch traced here: 81.8 us
  Pallas kernels  78.1 us (95%)
  local copies, waits for them, and re-layouts  2.31 us (3%)
  between operations  1.36 us (2%)
    pallas_call x1, Pallas kernels, on_device(): pl.pallas_call(kernel, out_shape=(jax.ShapeDtypeStruct((ROWS, HEAD), BF16...  73.8 us
    pallas_call x1, Pallas kernels, on_device(): pl.pallas_call(update, out_shape=jax.ShapeDtypeStruct((OWNED, HEAD, HEAD)...  4.34 us
    unnamed x13, local copies, waits for them, and re-layouts  2.31 us

profile of v1, /device:TPU:1, one launch (start us, length us, event | category | flops | bytes accessed | tf_op | source)
XLA Modules:
  0.0 81.8 jit_solution(11229730607511850653)
XLA Ops:
  1.3 0.0 copy-start
  1.3 0.0 copy-start.2
  1.3 0.0 copy-start.3
  1.3 0.0 copy-start.4
  1.3 73.8 %shard_map.113 = (bf16[512,256]{1,0:T(8,128)(2,1)}, bf16[4,2,2,256,256]{4,3,2,1,0:T(8,128)(2,1)}) custom-call(bf16[512,256]{1,0:T(8,128)(2,1)} %tokens.1, bf16[4,4,2,256,256]{4,3,2,1,0:T(8,128)(2,1)} %bitcast.11, bf16[4,4,2,256,256]{4,3,2,1,0:T(8,128)(2,1)} %bitcast.12, bf16[4,4,2,256,256]{4,3,2,1,0:T(8,128)(2,1)} %bitcast.13, ...), custom_call_target="tpu_custom_call" | custom-call | flops 11000000512 | bytes 24000000 | tf_op jit(solution)/shard_map/pallas_call | solution.py:367
  75.1 0.0 copy-done
  75.1 0.0 copy-done.2
  75.1 0.0 copy-done.3
  75.1 0.0 copy-done.4
  75.2 0.0 copy-start.1
  75.2 1.6 %copy-done.1 = bf16[4,2,2,256,256]{4,3,2,1,0:T(8,128)(2,1)S(1)} copy-done((bf16[4,2,2,256,256]{4,3,2,1,0:T(8,128)(2,1)S(1)}, bf16[4,2,2,256,256]{4,3,2,1,0:T(8,128)(2,1)}, u32[]{:S(2)}) %copy-start.1) | copy-done | bytes 2097176
  76.7 0.0 copy-start.5
  76.7 4.3 %shard_map.114 = f32[8,256,256]{2,1,0:T(8,128)} custom-call(bf16[4,2,2,256,256]{4,3,2,1,0:T(8,128)(2,1)S(1)} %copy-done.1, f32[8,256,256]{2,1,0:T(8,128)S(1)} %bitcast.9, f32[1]{0:T(128)S(6)} %copy.14.decay, s32[32]{0:T(128)S(1)} %copy-done.2, s32[32]{0:T(128)S(1)} %copy-done.3, s32[32]{0:T(128)S(1)} %copy-done.4), custom_call_target="tpu_custom_call" | custom-call | flops 300000000 | bytes 6000000 | tf_op jit(solution)/shard_map/pallas_call | solution.py:400
  81.1 0.0 copy-done.5
  81.1 0.7 copy.15
Async XLA Ops:
  1.3 73.8 %copy-start = (f32[8,1,256,256]{3,2,1,0:T(8,128)S(1)}, f32[8,1,256,256]{3,2,1,0:T(8,128)}, u32[]{:S(2)}) copy-start(f32[8,1,256,256]{3,2,1,0:T(8,128)} %param.16) | copy-start | bytes 6291460
  1.3 73.8 %copy-start.2 = (s32[32]{0:T(128)S(1)}, s32[32]{0:T(128)}, u32[]{:S(2)}) copy-start(s32[32]{0:T(128)} %lengths.3) | copy-start | bytes 388
  1.3 73.8 %copy-start.3 = (s32[32]{0:T(128)S(1)}, s32[32]{0:T(128)}, u32[]{:S(2)}) copy-start(s32[32]{0:T(128)} %slot_of.3) | copy-start | bytes 388
  1.3 73.8 %copy-start.4 = (s32[32]{0:T(128)S(1)}, s32[32]{0:T(128)}, u32[]{:S(2)}) copy-start(s32[32]{0:T(128)} %serve.3) | copy-start | bytes 388
  75.2 1.6 %copy-start.1 = (bf16[4,2,2,256,256]{4,3,2,1,0:T(8,128)(2,1)S(1)}, bf16[4,2,2,256,256]{4,3,2,1,0:T(8,128)(2,1)}, u32[]{:S(2)}) copy-start(bf16[4,2,2,256,256]{4,3,2,1,0:T(8,128)(2,1)} %get-tuple-element.5.keyval) | copy-start | bytes 6291460
  76.7 4.3 %copy-start.5 = (bf16[512,256]{1,0:T(8,128)(2,1)S(1)}, bf16[512,256]{1,0:T(8,128)(2,1)}, u32[]{:S(2)}) copy-start(bf16[512,256]{1,0:T(8,128)(2,1)} %get-tuple-element.10) | copy-start | bytes 786436

commit v2 on v1

--- a/solution.py
+++ b/solution.py
@@ -16,6 +16,7 @@
 CHUNKS = 2
 CHUNK = ROWS // CHUNKS
 PER = CHUNK // 128
+STAGGER = 4.5
 EPSILON = 1e-05
 F32 = jnp.float32
 BF16 = jnp.bfloat16
@@ -33,8 +34,8 @@
     (
         weights, prior_own, query, gate, total, starts,
         token_sem, pool_sem, weight_sem, out_sem,
-        near_send, near_recv, far_send, far_recv, twin_send, twin_recv,
-        state_send, state_recv, kv_send, kv_recv, relay_send, relay_recv,
+        near_send, near_recv, near2_send, near2_recv, far_send, far_recv, far2_send, far2_recv,
+        twin_send, twin_recv, state_send, state_recv, kv_send, kv_recv, relay_send, relay_recv,
     ) = scratch
     me = lax.axis_index("pool")
     place = lax.axis_index("tp")
@@ -86,31 +87,79 @@
             for which in range(4):
                 weight_copy(plane, line, which).start()
 
-    partners = [at(u + d, v) for d in (1, 2, 3)] + [at(u, v + d) for d in (1, 2, 3)]
+    partners = [at(u + 1, v), at(u - 1, v), at(u, v + 1), at(u, v - 1)]
     partners += [twin] + [group(d) for d in (1, 2, 3)]
     barrier = pltpu.get_barrier_semaphore()
     for partner in partners:
         pl.semaphore_signal(barrier, inc=1, device_id=partner, device_id_type=MESH)
     pl.semaphore_wait(barrier, len(partners))
 
-    def near(r, d):
-        return remote(
-            lines[r][0].at[0], lines[r][0].at[d],
-            near_send.at[r, d - 1], near_recv.at[r, d - 1], at(u + d, v),
-        )
-
-    def far(r, d):
-        return remote(
-            lines[r][0], lines[r][d], far_send.at[r, d - 1], far_recv.at[r, d - 1], at(u, v + d)
-        )
-
-    def to_twin(r, d):
-        return remote(lines[r][d], twins[r][d], twin_send.at[r, d], twin_recv.at[r, d], twin)
+    halves = (pl.ds(0, CHUNK // 2), pl.ds(CHUNK // 2, CHUNK // 2))
+
+    def near(r, way):
+        return remote(
+            lines[r][0].at[0], lines[r][0].at[1 + 2 * way],
+            near_send.at[r, way], near_recv.at[r, way], at(u + 1 - 2 * way, v),
+        )
+
+    def near2(r, way):
+        return remote(
+            lines[r][0].at[1 + 2 * way, halves[way]], lines[r][0].at[2, halves[way]],
+            near2_send.at[r, way], near2_recv.at[r, way], at(u + 1 - 2 * way, v),
+        )
+
+    def far(r, i, way):
+        return remote(
+            lines[r][0].at[i], lines[r][1 + 2 * way].at[i],
+            far_send.at[r, i, way], far_recv.at[r, i, way], at(u, v + 1 - 2 * way),
+        )
+
+    def far2(r, i, way):
+        return remote(
+            lines[r][1 + 2 * way].at[i, halves[way]], lines[r][2].at[i, halves[way]],
+            far2_send.at[r, i, way], far2_recv.at[r, i, way], at(u, v + 1 - 2 * way),
+        )
+
+    def to_twin(r, d, i):
+        return remote(
+            lines[r][d].at[i], twins[r][d].at[i], twin_send.at[r, d, i], twin_recv.at[r, d, i], twin
+        )
+
+    def spread(r, i):
+        for way in range(2):
+            far(r, i, way).start()
+        to_twin(r, 0, i).start()
+
+    def open_chunk(r):
+        token_copies[r].wait()
+        for way in range(2):
+            near(r, way).start()
+        spread(r, 0)
+
+    def near_in(r):
+        for way in range(2):
+            near(r, way).wait_recv()
+            near2(r, way).start()
+            spread(r, 1 + 2 * way)
+
+    def near2_in(r):
+        for way in range(2):
+            near2(r, way).wait_recv()
+        spread(r, 2)
+
+    def far_in(r, i):
+        for way in range(2):
+            far(r, i, way).wait_recv()
+            far2(r, i, way).start()
+            to_twin(r, 1 + 2 * way, i).start()
+
+    def far2_in(r, i):
+        for way in range(2):
+            far2(r, i, way).wait_recv()
+        to_twin(r, 2, i).start()
 
     for r in range(CHUNKS):
-        token_copies[r].wait()
-        for d in (1, 3, 2):
-            near(r, d).start()
+        open_chunk(r)
 
     zero = jnp.int32(0)
 
@@ -158,30 +207,35 @@
     for k in range(SLOTS):
         prior[0][k] = prior_own[(own_rows[0] >> (3 * k)) & 7].astype(BF16)
 
-    def send_far(r):
-        for d in (1, 2, 3):
-            near(r, d).wait_recv()
-        for d in (1, 3, 2):
-            far(r, d).start()
-
-    def multiply(part, plane, line, first):
+    def multiply(part, plane, line, first, r, pair):
         left = jnp.concatenate([part[i] for i in range(4)], axis=1)
 
-        def one(which, _):
+        def one(n, _):
+            which = 1 + n if pair == 0 else 3 * n
             right = jnp.concatenate(
                 [weights[plane, line, which, (first - i + 4) % 4] for i in range(4)], axis=0
             )
-            total[which] += jnp.dot(left, right, preferred_element_type=F32)
+            total[r, n] += jnp.dot(left, right, preferred_element_type=F32)
             return 0
 
-        lax.fori_loop(0, 4, one, 0)
+        lax.fori_loop(0, 2, one, 0, unroll=True)
+
+    def own(r, d, pair=0):
+        multiply(lines[r][d], core, (v - d + 4) % 4, u, r, pair)
+
+    def other(r, d, pair=0):
+        if pair == 0:
+            for i in range(4):
+                to_twin(r, d, i).wait_recv()
+        multiply(twins[r][d], 1 - core, (u - d + 4) % 4, v, r, pair)
 
     def side(way):
         return group(1 if way == 0 else -1)
 
-    def kv_out(r, way):
-        return remote(
-            keyval[0].at[r], keyval[1 + way].at[r], kv_send.at[r, way], kv_recv.at[r, way], side(way)
+    def kv_out(r, way, which):
+        return remote(
+            keyval[0].at[r, which], keyval[1 + way].at[r, which],
+            kv_send.at[r, way, which], kv_recv.at[r, way, which], side(way),
         )
 
     def relay(r, way):
@@ -190,36 +244,50 @@
             relay_send.at[r, way], relay_recv.at[r, way], side(way),
         )
 
-    send_far(0)
-    for line in range(4):
-        for plane in range(2):
-            for which in range(4):
-                weight_copy(plane, line, which).wait()
-
-    for r in range(CHUNKS):
-        total[...] = jnp.zeros_like(total)
-        for j, d in enumerate((0, 1, 3, 2)):
-            if j > 0:
-                far(r, d).wait_recv()
-            to_twin(r, d).start()
-            if j == 2 and r + 1 < CHUNKS:
-                send_far(r + 1)
-            multiply(lines[r][d], core, (v - d + 4) % 4, u)
-            to_twin(r, d).wait_recv()
-            multiply(twins[r][d], 1 - core, (u - d + 4) % 4, v)
-        query[r * CHUNK:(r + 1) * CHUNK, :] = total[0].astype(BF16)
-        keyval[0][r, 0] = (total[1] * HEAD ** (-0.5)).astype(BF16)
-        keyval[0][r, 1] = total[2].astype(BF16)
-        gate[r * CHUNK:(r + 1) * CHUNK, :] = total[3].astype(BF16)
-        kv_out(r, 0).start()
-        kv_out(r, 1).start()
+    def finish(r):
+        keyval[0][r, 0] = (total[r, 0] * HEAD ** (-0.5)).astype(BF16)
+        kv_out(r, 0, 0).start()
+        keyval[0][r, 1] = total[r, 1].astype(BF16)
+        kv_out(r, 1, 1).start()
+        kv_out(r, 0, 1).start()
+        kv_out(r, 1, 0).start()
 
     def pass_on(r):
         for way in range(2):
-            kv_out(r, way).wait_recv()
+            kv_out(r, way, way).wait_recv()
             relay(r, way).start()
 
-    pass_on(0)
+    def rest(r):
+        total[r] = jnp.zeros_like(total[r])
+        for d in range(4):
+            own(r, d, 1)
+            other(r, d, 1)
+        query[r * CHUNK:(r + 1) * CHUNK, :] = total[r, 0].astype(BF16)
+        gate[r * CHUNK:(r + 1) * CHUNK, :] = total[r, 1].astype(BF16)
+
+    def get_weights(_):
+        for line in range(4):
+            for plane in range(2):
+                for which in range(4):
+                    weight_copy(plane, line, which).wait()
+
+    steps = [
+        (1, near_in), (2, far_in, 0), (3, near2_in), (4, far_in, 1), (5, far_in, 3), (6, far_in, 2),
+        (7, far2_in, 0), (8, far2_in, 1), (9, far2_in, 3), (10, far2_in, 2),
+        (6.5, own, 0), (7.5, other, 0), (8.2, own, 1), (8.7, own, 3), (9.5, other, 1),
+        (9.7, other, 3), (10.5, own, 2), (11, other, 2), (11.5, finish),
+    ]
+    total[...] = jnp.zeros_like(total)
+    order = [(when + STAGGER * r, r, *step) for r in range(CHUNKS) for when, *step in steps]
+    order.append((6.4, 0, get_weights))
+    for _, r, step, *more in sorted(order, key=lambda entry: entry[:2]):
+        if step is finish and r > 0:
+            pass_on(r - 1)
+        step(r, *more)
+    rest(0)
+    pass_on(CHUNKS - 1)
+    for r in range(1, CHUNKS):
+        rest(r)
 
     for k in range(SLOTS):
         for d in (1, 2, 3):
@@ -276,8 +344,9 @@
         return 0
 
     lax.fori_loop(0, CHUNKS, retain, 0)
-    for r in range(1, CHUNKS):
-        pass_on(r)
+    for r in range(CHUNKS):
+        for way in range(2):
+            kv_out(r, way, 1 - way).wait_recv()
     for r in range(CHUNKS):
         for way in range(2):
             relay(r, way).wait_recv()
@@ -287,13 +356,17 @@
     for copy in out_copies:
         copy.start()
     for r in range(CHUNKS):
-        for d in (1, 2, 3):
-            near(r, d).wait_send()
-            far(r, d).wait_send()
-        for d in range(4):
-            to_twin(r, d).wait_send()
-        for way in range(2):
-            kv_out(r, way).wait_send()
+        for i in range(4):
+            for d in range(4):
+                to_twin(r, d, i).wait_send()
+            for way in range(2):
+                far(r, i, way).wait_send()
+                far2(r, i, way).wait_send()
+        for way in range(2):
+            near(r, way).wait_send()
+            near2(r, way).wait_send()
+            for which in range(2):
+                kv_out(r, way, which).wait_send()
             relay(r, way).wait_send()
     for k in range(SLOTS):
         for d in (1, 2, 3):
@@ -380,14 +453,14 @@
             pltpu.VMEM((OWNED, HEAD, HEAD), F32),
             pltpu.VMEM((ROWS, HEAD), BF16),
             pltpu.VMEM((ROWS, HEAD), BF16),
-            pltpu.VMEM((4, CHUNK, HEAD), F32),
+            pltpu.VMEM((CHUNKS, 2, CHUNK, HEAD), F32),
             pltpu.SMEM((SESSIONS,), jnp.int32),
             dma((CHUNKS,)), dma, dma((2, 4, 4)), dma((4,)),
-            dma((CHUNKS, 3)), dma((CHUNKS, 3)),
-            dma((CHUNKS, 3)), dma((CHUNKS, 3)),
-            dma((CHUNKS, 4)), dma((CHUNKS, 4)),
+            *[dma((CHUNKS, 2))] * 4,
+            *[dma((CHUNKS, 4, 2))] * 4,
+            *[dma((CHUNKS, 4, 4))] * 2,
             dma((3, SLOTS)), dma((3, SLOTS)),
-            dma((CHUNKS, 2)), dma((CHUNKS, 2)),
+            dma((CHUNKS, 2, 2)), dma((CHUNKS, 2, 2)),
             dma((CHUNKS, 2)), dma((CHUNKS, 2)),
         ],
         compiler_params=pltpu.CompilerParams(

time: 82 us -> 65.3 us (0.80)
  Pallas kernels: 78.1 us -> 61.4 us
    pallas_call x1, Pallas kernels: 73.8 us -> 57 us  [on_device(): pl.pallas_call(kernel, out_shape=(jax.ShapeDtypeStruct((ROWS, HEAD), BF16...]
where the time goes in v2:
time: 65.3 us; the launch traced here: 65.1 us
  Pallas kernels  61.4 us (94%)
  local copies, waits for them, and re-layouts  2.31 us (4%)
  between operations  1.36 us (2%)
    pallas_call x1, Pallas kernels, on_device(): pl.pallas_call(kernel, out_shape=(jax.ShapeDtypeStruct((ROWS, HEAD), BF16...  57 us
    pallas_call x1, Pallas kernels, on_device(): pl.pallas_call(update, out_shape=jax.ShapeDtypeStruct((OWNED, HEAD, HEAD)...  4.34 us
    unnamed x13, local copies, waits for them, and re-layouts  2.31 us

profile of v2, /device:TPU:1, one launch (start us, length us, event | category | flops | bytes accessed | tf_op | source)
XLA Modules:
  0.0 65.1 jit_solution(5856035499238980243)
XLA Ops:
  1.3 0.0 copy-start
  1.3 0.0 copy-start.2
  1.3 0.0 copy-start.3
  1.3 0.0 copy-start.4
  1.3 57.0 %shard_map.113 = (bf16[512,256]{1,0:T(8,128)(2,1)}, bf16[4,2,2,256,256]{4,3,2,1,0:T(8,128)(2,1)}) custom-call(bf16[512,256]{1,0:T(8,128)(2,1)} %tokens.1, bf16[4,4,2,256,256]{4,3,2,1,0:T(8,128)(2,1)} %bitcast.11, bf16[4,4,2,256,256]{4,3,2,1,0:T(8,128)(2,1)} %bitcast.12, bf16[4,4,2,256,256]{4,3,2,1,0:T(8,128)(2,1)} %bitcast.13, ...), custom_call_target="tpu_custom_call" | custom-call | flops 11000000512 | bytes 24000000 | tf_op jit(solution)/shard_map/pallas_call | solution.py:440
  58.4 0.0 copy-done
  58.4 0.0 copy-done.2
  58.4 0.0 copy-done.3
  58.4 0.0 copy-done.4
  58.4 0.0 copy-start.1
  58.4 1.6 %copy-done.1 = bf16[4,2,2,256,256]{4,3,2,1,0:T(8,128)(2,1)S(1)} copy-done((bf16[4,2,2,256,256]{4,3,2,1,0:T(8,128)(2,1)S(1)}, bf16[4,2,2,256,256]{4,3,2,1,0:T(8,128)(2,1)}, u32[]{:S(2)}) %copy-start.1) | copy-done | bytes 2097176
  60.0 0.0 copy-start.5
  60.0 4.3 %shard_map.114 = f32[8,256,256]{2,1,0:T(8,128)} custom-call(bf16[4,2,2,256,256]{4,3,2,1,0:T(8,128)(2,1)S(1)} %copy-done.1, f32[8,256,256]{2,1,0:T(8,128)S(1)} %bitcast.9, f32[1]{0:T(128)S(6)} %copy.14.decay, s32[32]{0:T(128)S(1)} %copy-done.2, s32[32]{0:T(128)S(1)} %copy-done.3, s32[32]{0:T(128)S(1)} %copy-done.4), custom_call_target="tpu_custom_call" | custom-call | flops 300000000 | bytes 6000000 | tf_op jit(solution)/shard_map/pallas_call | solution.py:473
  64.3 0.0 copy-done.5
  64.3 0.7 %copy.15 = bf16[512,256]{1,0:T(8,128)(2,1)} copy(bf16[512,256]{1,0:T(8,128)(2,1)S(1)} %copy-done.5) | data formatting | bytes 524288
Async XLA Ops:
  1.3 57.1 %copy-start = (f32[8,1,256,256]{3,2,1,0:T(8,128)S(1)}, f32[8,1,256,256]{3,2,1,0:T(8,128)}, u32[]{:S(2)}) copy-start(f32[8,1,256,256]{3,2,1,0:T(8,128)} %param.16) | copy-start | bytes 6291460
  1.3 57.1 %copy-start.2 = (s32[32]{0:T(128)S(1)}, s32[32]{0:T(128)}, u32[]{:S(2)}) copy-start(s32[32]{0:T(128)} %lengths.3) | copy-start | bytes 388
  1.3 57.1 %copy-start.3 = (s32[32]{0:T(128)S(1)}, s32[32]{0:T(128)}, u32[]{:S(2)}) copy-start(s32[32]{0:T(128)} %slot_of.3) | copy-start | bytes 388
  1.3 57.1 %copy-start.4 = (s32[32]{0:T(128)S(1)}, s32[32]{0:T(128)}, u32[]{:S(2)}) copy-start(s32[32]{0:T(128)} %serve.3) | copy-start | bytes 388
  58.4 1.6 %copy-start.1 = (bf16[4,2,2,256,256]{4,3,2,1,0:T(8,128)(2,1)S(1)}, bf16[4,2,2,256,256]{4,3,2,1,0:T(8,128)(2,1)}, u32[]{:S(2)}) copy-start(bf16[4,2,2,256,256]{4,3,2,1,0:T(8,128)(2,1)} %get-tuple-element.5.keyval) | copy-start | bytes 6291460
  60.0 4.3 %copy-start.5 = (bf16[512,256]{1,0:T(8,128)(2,1)S(1)}, bf16[512,256]{1,0:T(8,128)(2,1)}, u32[]{:S(2)}) copy-start(bf16[512,256]{1,0:T(8,128)(2,1)} %get-tuple-element.10) | copy-start | bytes 786436

commit v3 on v2

--- a/solution.py
+++ b/solution.py
@@ -13,9 +13,14 @@
 SESSIONS = 32
 OWNED = 8
 SLOTS = 4
-CHUNKS = 2
-CHUNK = ROWS // CHUNKS
-PER = CHUNK // 128
+LMAX = 128
+SIZES = (256, 256)
+CHUNKS = len(SIZES)
+FIRST = tuple(sum(SIZES[:n]) for n in range(CHUNKS))
+PART = 64
+PARTS = ROWS // PART
+SPAN = LMAX // PART + 1
+BAND = 256
 STAGGER = 4.5
 EPSILON = 1e-05
 F32 = jnp.float32
@@ -24,15 +29,16 @@
 
 def kernel(
     tokens, w_query, w_key, w_value, w_gate, pool, decay, lengths, slot_of, serve,
-    retained, keyval_out, *scratch,
+    retained, new_states, *scratch,
 ):
     lines = [scratch[4 * r:4 * r + 4] for r in range(CHUNKS)]
     scratch = scratch[4 * CHUNKS:]
     twins = [scratch[4 * r:4 * r + 4] for r in range(CHUNKS)]
     scratch = scratch[4 * CHUNKS:]
     prior, packed, keyval, scratch = scratch[:4], scratch[4:7], scratch[7:11], scratch[11:]
+    total, scratch = scratch[:CHUNKS], scratch[CHUNKS:]
     (
-        weights, prior_own, query, gate, total, starts,
+        weights, prior_own, fresh, query, gate, starts,
         token_sem, pool_sem, weight_sem, out_sem,
         near_send, near_recv, near2_send, near2_recv, far_send, far_recv, far2_send, far2_recv,
         twin_send, twin_recv, state_send, state_recv, kv_send, kv_recv, relay_send, relay_recv,
@@ -61,11 +67,11 @@
         )
 
     def rows_of(r):
-        return pl.ds(pl.multiple_of(r * CHUNK, CHUNK), CHUNK)
+        return pl.ds(FIRST[r], SIZES[r])
 
     token_copies = [
         pltpu.make_async_copy(
-            tokens.at[pl.ds(r * CHUNK, CHUNK)], lines[r][0].at[0], token_sem.at[r]
+            tokens.at[rows_of(r)], lines[r][0].at[0], token_sem.at[r]
         )
         for r in range(CHUNKS)
     ]
@@ -87,14 +93,15 @@
             for which in range(4):
                 weight_copy(plane, line, which).start()
 
-    partners = [at(u + 1, v), at(u - 1, v), at(u, v + 1), at(u, v - 1)]
+    partners = [at(u + 1, v), at(u - 1, v), at(u + 2, v), at(u, v + 1), at(u, v - 1)]
     partners += [twin] + [group(d) for d in (1, 2, 3)]
     barrier = pltpu.get_barrier_semaphore()
     for partner in partners:
         pl.semaphore_signal(barrier, inc=1, device_id=partner, device_id_type=MESH)
     pl.semaphore_wait(barrier, len(partners))
 
-    halves = (pl.ds(0, CHUNK // 2), pl.ds(CHUNK // 2, CHUNK // 2))
+    def half(r, way):
+        return pl.ds(way * (SIZES[r] // 2), SIZES[r] // 2)
 
     def near(r, way):
         return remote(
@@ -102,10 +109,9 @@
             near_send.at[r, way], near_recv.at[r, way], at(u + 1 - 2 * way, v),
         )
 
-    def near2(r, way):
-        return remote(
-            lines[r][0].at[1 + 2 * way, halves[way]], lines[r][0].at[2, halves[way]],
-            near2_send.at[r, way], near2_recv.at[r, way], at(u + 1 - 2 * way, v),
+    def near2(r):
+        return remote(
+            lines[r][0].at[0], lines[r][0].at[2], near2_send.at[r], near2_recv.at[r], at(u + 2, v)
         )
 
     def far(r, i, way):
@@ -116,7 +122,7 @@
 
     def far2(r, i, way):
         return remote(
-            lines[r][1 + 2 * way].at[i, halves[way]], lines[r][2].at[i, halves[way]],
+            lines[r][1 + 2 * way].at[i, half(r, way)], lines[r][2].at[i, half(r, way)],
             far2_send.at[r, i, way], far2_recv.at[r, i, way], at(u, v + 1 - 2 * way),
         )
 
@@ -134,17 +140,16 @@
         token_copies[r].wait()
         for way in range(2):
             near(r, way).start()
+        near2(r).start()
         spread(r, 0)
 
     def near_in(r):
         for way in range(2):
             near(r, way).wait_recv()
-            near2(r, way).start()
             spread(r, 1 + 2 * way)
 
     def near2_in(r):
-        for way in range(2):
-            near2(r, way).wait_recv()
+        near2(r).wait_recv()
         spread(r, 2)
 
     def far_in(r, i):
@@ -164,7 +169,7 @@
     zero = jnp.int32(0)
 
     def scan(s, carry):
-        own_rows, own_count, ids, id_count, run = carry
+        own_rows, own_count, ids, id_count, run, inverse = carry
         slot, to, long = slot_of[s], serve[s], lengths[s]
         owner, row = slot // OWNED, slot % OWNED
         begin = zero
@@ -186,11 +191,12 @@
         return (
             tuple(own_rows_n), tuple(own_count_n), tuple(ids_n), tuple(id_count_n),
             tuple(new_run),
+            tuple(jnp.where(mine & (row == i), s, inverse[i]) for i in range(OWNED)),
         )
 
     four = (zero,) * 4
-    own_rows, _, ids, id_count, _ = lax.fori_loop(
-        0, SESSIONS, scan, (four, four, four, four, four)
+    own_rows, _, ids, id_count, _, inverse = lax.fori_loop(
+        0, SESSIONS, scan, (four, four, four, four, four, (zero,) * OWNED)
     )
 
     def state(d, k):
@@ -215,7 +221,7 @@
             right = jnp.concatenate(
                 [weights[plane, line, which, (first - i + 4) % 4] for i in range(4)], axis=0
             )
-            total[r, n] += jnp.dot(left, right, preferred_element_type=F32)
+            total[r][n] += jnp.dot(left, right, preferred_element_type=F32)
             return 0
 
         lax.fori_loop(0, 2, one, 0, unroll=True)
@@ -232,22 +238,26 @@
     def side(way):
         return group(1 if way == 0 else -1)
 
+    def parts_of(r):
+        return pl.ds(FIRST[r] // PART, SIZES[r] // PART)
+
     def kv_out(r, way, which):
         return remote(
-            keyval[0].at[r, which], keyval[1 + way].at[r, which],
+            keyval[0].at[which, parts_of(r)], keyval[1 + way].at[which, parts_of(r)],
             kv_send.at[r, way, which], kv_recv.at[r, way, which], side(way),
         )
 
     def relay(r, way):
         return remote(
-            keyval[1 + way].at[r, way], keyval[3].at[r, way],
+            keyval[1 + way].at[way, parts_of(r)], keyval[3].at[way, parts_of(r)],
             relay_send.at[r, way], relay_recv.at[r, way], side(way),
         )
 
     def finish(r):
-        keyval[0][r, 0] = (total[r, 0] * HEAD ** (-0.5)).astype(BF16)
+        shape = (SIZES[r] // PART, PART, HEAD)
+        keyval[0][0, parts_of(r)] = (total[r][0] * HEAD ** (-0.5)).astype(BF16).reshape(shape)
         kv_out(r, 0, 0).start()
-        keyval[0][r, 1] = total[r, 1].astype(BF16)
+        keyval[0][1, parts_of(r)] = total[r][1].astype(BF16).reshape(shape)
         kv_out(r, 1, 1).start()
         kv_out(r, 0, 1).start()
         kv_out(r, 1, 0).start()
@@ -258,12 +268,12 @@
             relay(r, way).start()
 
     def rest(r):
-        total[r] = jnp.zeros_like(total[r])
+        total[r][...] = jnp.zeros_like(total[r])
         for d in range(4):
             own(r, d, 1)
             other(r, d, 1)
-        query[r * CHUNK:(r + 1) * CHUNK, :] = total[r, 0].astype(BF16)
-        gate[r * CHUNK:(r + 1) * CHUNK, :] = total[r, 1].astype(BF16)
+        query[rows_of(r), :] = total[r][0].astype(BF16)
+        gate[rows_of(r), :] = total[r][1].astype(BF16)
 
     def get_weights(_):
         for line in range(4):
@@ -277,7 +287,8 @@
         (6.5, own, 0), (7.5, other, 0), (8.2, own, 1), (8.7, own, 3), (9.5, other, 1),
         (9.7, other, 3), (10.5, own, 2), (11, other, 2), (11.5, finish),
     ]
-    total[...] = jnp.zeros_like(total)
+    for r in range(CHUNKS):
+        total[r][...] = jnp.zeros_like(total[r])
     order = [(when + STAGGER * r, r, *step) for r in range(CHUNKS) for when, *step in steps]
     order.append((6.4, 0, get_weights))
     for _, r, step, *more in sorted(order, key=lambda entry: entry[:2]):
@@ -303,14 +314,14 @@
             last.append(jnp.where(k < id_count[g], starts[s] + lengths[s], 0))
 
     def own_rows_of(which):
-        return jnp.concatenate([keyval[0][n, which] for n in range(CHUNKS)], axis=0)
+        return keyval[0][which].reshape(ROWS, HEAD)
 
     def retain(r, _):
-        row = lax.broadcasted_iota(jnp.int32, (CHUNK, 1), 0) + r * CHUNK
-        live = jnp.zeros((CHUNK, 1), jnp.bool_)
-        begin = jnp.full((CHUNK, 1), ROWS, jnp.int32)
-        q = query[rows_of(r), :]
-        carried = jnp.zeros((CHUNK, HEAD), F32)
+        rows = pl.ds(pl.multiple_of(r * BAND, BAND), BAND)
+        row = lax.broadcasted_iota(jnp.int32, (BAND, 1), 0) + r * BAND
+        begin = jnp.full((BAND, 1), ROWS, jnp.int32)
+        q = query[rows, :]
+        carried = jnp.zeros((BAND, HEAD), F32)
         for g in range(4):
             parts = []
             for k in range(SLOTS):
@@ -323,7 +334,7 @@
                 preferred_element_type=F32,
             )
         live = begin < ROWS
-        column = lax.broadcasted_iota(jnp.int32, (CHUNK, ROWS), 1)
+        column = lax.broadcasted_iota(jnp.int32, (BAND, ROWS), 1)
         distance = row - column
         scores = lax.dot_general(
             q, own_rows_of(0), (((1,), (1,)), ((), ())), preferred_element_type=F32
@@ -338,23 +349,46 @@
         centered = mixed - jnp.mean(mixed, axis=-1, keepdims=True)
         variance = jnp.mean(centered * centered, axis=-1, keepdims=True)
         normed = centered * lax.rsqrt(variance + EPSILON)
-        out = gate[rows_of(r), :].astype(F32)
+        out = gate[rows, :].astype(F32)
         out = out * (1.0 / (1.0 + jnp.exp(-out))) * normed
-        retained[rows_of(r), :] = jnp.where(live, out, 0.0).astype(BF16)
+        retained[rows, :] = jnp.where(live, out, 0.0).astype(BF16)
         return 0
 
-    lax.fori_loop(0, CHUNKS, retain, 0)
+    lax.fori_loop(0, ROWS // BAND, retain, 0)
     for r in range(CHUNKS):
         for way in range(2):
             kv_out(r, way, 1 - way).wait_recv()
     for r in range(CHUNKS):
         for way in range(2):
             relay(r, way).wait_recv()
-    out_copies = [
-        pltpu.make_async_copy(keyval[n], keyval_out.at[n], out_sem.at[n]) for n in range(4)
-    ]
-    for copy in out_copies:
-        copy.start()
+    out_copies = []
+    for i in range(OWNED):
+        s = inverse[i]
+        begin, long = starts[s], lengths[s]
+        away = (me - serve[s] + 4) % 4
+        low = jnp.minimum(begin // PART, PARTS - SPAN)
+        row = lax.broadcasted_iota(jnp.int32, (SPAN * PART, 1), 0) + low * PART
+        behind = begin + long - 1 - row
+        tail = jnp.exp(jnp.maximum(behind, 0).astype(F32) * log_gamma)
+        tail = jnp.where((row >= begin) & (behind >= 0), tail, 0.0)
+
+        def turn_rows(which):
+            blocks = []
+            for n in range(SPAN):
+                block = keyval[0][which, low + n]
+                for place, group_away in ((1, 1), (2, 3), (3, 2)):
+                    block = jnp.where(away == group_away, keyval[place][which, low + n], block)
+                blocks.append(block)
+            return jnp.concatenate(blocks, axis=0)
+
+        change = lax.dot_general(
+            (turn_rows(0).astype(F32) * tail).astype(BF16), turn_rows(1),
+            (((0,), (0,)), ((), ())), preferred_element_type=F32,
+        )
+        keep = jnp.exp(jnp.full((1, 1), long, jnp.int32).astype(F32) * log_gamma)
+        fresh[i] = keep * prior_own[i] + change
+        out_copies.append(pltpu.make_async_copy(fresh.at[i], new_states.at[i], out_sem.at[i]))
+        out_copies[i].start()
     for r in range(CHUNKS):
         for i in range(4):
             for d in range(4):
@@ -362,9 +396,9 @@
             for way in range(2):
                 far(r, i, way).wait_send()
                 far2(r, i, way).wait_send()
+        near2(r).wait_send()
         for way in range(2):
             near(r, way).wait_send()
-            near2(r, way).wait_send()
             for which in range(2):
                 kv_out(r, way, which).wait_send()
             relay(r, way).wait_send()
@@ -375,59 +409,22 @@
         copy.wait()
 
 
-def update(keyval, pool, decay, lengths, slot_of, serve, new_states, starts):
-    me = lax.axis_index("pool")
-    zero = jnp.int32(0)
-
-    def scan(s, run):
-        to = serve[s]
-        begin = zero
-        for g in range(4):
-            begin = jnp.where(to == g, run[g], begin)
-        slot = slot_of[s]
-
-        @pl.when(slot // OWNED == me)
-        def _():
-            away = (me - to + 4) % 4
-            starts[0, slot % OWNED] = jnp.where(away == 3, 2, jnp.where(away == 2, 3, away))
-            starts[1, slot % OWNED] = begin
-            starts[2, slot % OWNED] = lengths[s]
-
-        return tuple(run[g] + jnp.where(to == g, lengths[s], 0) for g in range(4))
-
-    lax.fori_loop(0, SESSIONS, scan, (zero,) * 4)
-    log_gamma = jnp.log(jnp.full((1, 1), decay[0], F32))
-
-    def one(i, _):
-        place, begin, long = starts[0, i], starts[1, i], starts[2, i]
-        low = jnp.minimum(begin // 128, ROWS // 128 - 2)
-        row = lax.broadcasted_iota(jnp.int32, (256, 1), 0) + low * 128
-
-        def rows_at(which):
-            return jnp.concatenate(
-                [
-                    keyval[
-                        place, (low + n) // PER, which,
-                        pl.ds(pl.multiple_of((low + n) % PER * 128, 128), 128), :,
-                    ]
-                    for n in range(2)
-                ],
-                axis=0,
-            )
-
-        behind = begin + long - 1 - row
-        tail = jnp.exp(jnp.maximum(behind, 0).astype(F32) * log_gamma)
-        tail = jnp.where((row >= begin) & (behind >= 0), tail, 0.0)
-        k_rows = rows_at(0).astype(F32) * tail
-        v_rows = rows_at(1)
-        change = lax.dot_general(
-            k_rows.astype(BF16), v_rows, (((0,), (0,)), ((), ())), preferred_element_type=F32
-        )
-        keep = jnp.exp(jnp.full((1, 1), long, jnp.int32).astype(F32) * log_gamma)
-        new_states[i] = keep * pool[i] + change
-        return 0
-
-    lax.fori_loop(0, OWNED, one, 0, unroll=2)
+def deliver(retained, new_states, retained_out, new_states_out, rows, states, sem):
+    passes = [(retained, rows, retained_out)]
+    passes += [(new_states.at[i], states.at[i], new_states_out.at[i]) for i in range(OWNED)]
+    loads = [
+        pltpu.make_async_copy(src, held, sem.at[n, 0]) for n, (src, held, _) in enumerate(passes)
+    ]
+    stores = [
+        pltpu.make_async_copy(held, dst, sem.at[n, 1]) for n, (_, held, dst) in enumerate(passes)
+    ]
+    for load in loads:
+        load.start()
+    for load, store in zip(loads, stores):
+        load.wait()
+        store.start()
+    for store in stores:
+        store.wait()
 
 
 def on_device(tokens, w_query, w_key, w_value, w_gate, decay, pool_states, lengths, slot_of, serve):
@@ -437,26 +434,27 @@
     dma = pltpu.SemaphoreType.DMA
     split = [w.reshape(4, 4, 2, HEAD, HEAD) for w in (w_query, w_key, w_value, w_gate)]
     states = pool_states.reshape(OWNED, HEAD, HEAD)
-    retained, keyval = pl.pallas_call(
+    retained, new_states = pl.pallas_call(
         kernel,
         out_shape=(
             jax.ShapeDtypeStruct((ROWS, HEAD), BF16),
-            jax.ShapeDtypeStruct((4, CHUNKS, 2, CHUNK, HEAD), BF16),
+            jax.ShapeDtypeStruct((OWNED, HEAD, HEAD), F32),
         ),
         in_specs=[hbm] * 6 + [smem] * 4,
         out_specs=(vmem, hbm),
         scratch_shapes=[
-            *[pltpu.VMEM((4, CHUNK, HEAD), BF16)] * (8 * CHUNKS),
+            *[pltpu.VMEM((4, size, HEAD), BF16) for size in SIZES for _ in range(4)] * 2,
             *[pltpu.VMEM((SLOTS, HEAD, HEAD), BF16)] * 7,
-            *[pltpu.VMEM((CHUNKS, 2, CHUNK, HEAD), BF16)] * 4,
+            *[pltpu.VMEM((2, PARTS, PART, HEAD), BF16)] * 4,
+            *[pltpu.VMEM((2, size, HEAD), F32) for size in SIZES],
             pltpu.VMEM((2, 4, 4, 4, HEAD, HEAD), BF16),
-            pltpu.VMEM((OWNED, HEAD, HEAD), F32),
+            *[pltpu.VMEM((OWNED, HEAD, HEAD), F32)] * 2,
             pltpu.VMEM((ROWS, HEAD), BF16),
             pltpu.VMEM((ROWS, HEAD), BF16),
-            pltpu.VMEM((CHUNKS, 2, CHUNK, HEAD), F32),
             pltpu.SMEM((SESSIONS,), jnp.int32),
-            dma((CHUNKS,)), dma, dma((2, 4, 4)), dma((4,)),
-            *[dma((CHUNKS, 2))] * 4,
+            dma((CHUNKS,)), dma, dma((2, 4, 4)), dma((OWNED,)),
+            *[dma((CHUNKS, 2))] * 2,
+            *[dma((CHUNKS,))] * 2,
             *[dma((CHUNKS, 4, 2))] * 4,
             *[dma((CHUNKS, 4, 4))] * 2,
             dma((3, SLOTS)), dma((3, SLOTS)),
@@ -470,17 +468,20 @@
             flops=11_000_000_000, bytes_accessed=24_000_000, transcendentals=1_000_000
         ),
     )(tokens, *split, states, decay, lengths, slot_of, serve)
-    new_states = pl.pallas_call(
-        update,
-        out_shape=jax.ShapeDtypeStruct((OWNED, HEAD, HEAD), F32),
-        in_specs=[vmem, vmem] + [smem] * 4,
-        out_specs=vmem,
-        scratch_shapes=[pltpu.SMEM((3, OWNED), jnp.int32)],
-        compiler_params=pltpu.CompilerParams(vmem_limit_bytes=24 << 20),
-        cost_estimate=pl.CostEstimate(
-            flops=300_000_000, bytes_accessed=6_000_000, transcendentals=2048
+    retained, new_states = pl.pallas_call(
+        deliver,
+        out_shape=(
+            jax.ShapeDtypeStruct(retained.shape, BF16),
+            jax.ShapeDtypeStruct(new_states.shape, F32),
         ),
-    )(keyval, states, decay, lengths, slot_of, serve)
+        in_specs=[hbm, hbm],
+        out_specs=(hbm, hbm),
+        scratch_shapes=[
+            pltpu.VMEM(retained.shape, BF16),
+            pltpu.VMEM(new_states.shape, F32),
+            dma((OWNED + 1, 2)),
+        ],
+    )(retained, new_states)
     return retained, new_states.reshape(OWNED, 1, HEAD, HEAD)
 
 

time: 65.3 us -> 60.8 us (0.931)
  local copies, waits for them, and re-layouts: 2.31 us -> 0 us
  Pallas kernels: 61.4 us -> 59.3 us
    unnamed x13 -> x0, local copies, waits for them, and re-layouts: 2.31 us -> none
    pallas_call x1, Pallas kernels: 4.34 us -> 2.5 us  [on_device(): pl.pallas_call(deliver, out_shape=(jax.ShapeDtypeStruct(retained.shape, B...]
where the time goes in v3:
time: 60.8 us; the launch traced here: 60.6 us
  Pallas kernels  59.3 us (98%)
  between operations  1.29 us (2%)
    pallas_call x1, Pallas kernels, on_device(): pl.pallas_call(kernel, out_shape=(jax.ShapeDtypeStruct((ROWS, HEAD), BF16...  56.8 us
    pallas_call x1, Pallas kernels, on_device(): pl.pallas_call(deliver, out_shape=(jax.ShapeDtypeStruct(retained.shape, B...  2.5 us

profile of v3, /device:TPU:1, one launch (start us, length us, event | category | flops | bytes accessed | tf_op | source)
XLA Modules:
  0.0 60.6 jit_solution(3602072421276929152)
XLA Ops:
  1.3 56.8 %shard_map.113 = (bf16[512,256]{1,0:T(8,128)(2,1)}, f32[8,256,256]{2,1,0:T(8,128)}) custom-call(bf16[512,256]{1,0:T(8,128)(2,1)} %tokens.1, bf16[4,4,2,256,256]{4,3,2,1,0:T(8,128)(2,1)} %bitcast.8, bf16[4,4,2,256,256]{4,3,2,1,0:T(8,128)(2,1)} %bitcast.9, bf16[4,4,2,256,256]{4,3,2,1,0:T(8,128)(2,1)} %bitcast.10, bf16[4,4,2,256,256]{4,3,2,1,0:T(8,128)(2,1)} %bitcast.11, ...), custom_call_target="tpu_custom_call" | custom-call | flops 11000000512 | bytes 24000000 | tf_op jit(solution)/shard_map/pallas_call | solution.py:437
  58.1 2.5 %shard_map.114 = (bf16[512,256]{1,0:T(8,128)(2,1)}, f32[8,256,256]{2,1,0:T(8,128)}) custom-call(bf16[512,256]{1,0:T(8,128)(2,1)} %get-tuple-element.6.retained, f32[8,256,256]{2,1,0:T(8,128)} %get-tuple-element.7.new_states), custom_call_target="tpu_custom_call" | custom-call | tf_op jit(solution)/shard_map/pallas_call | solution.py:471

commit v4 on v3

--- a/solution.py
+++ b/solution.py
@@ -69,6 +69,12 @@
     def rows_of(r):
         return pl.ds(FIRST[r], SIZES[r])
 
+    partners = [at(u + 1, v), at(u - 1, v), at(u + 2, v), at(u, v + 1), at(u, v - 1)]
+    partners += [twin] + [group(d) for d in (1, 2, 3)]
+    barrier = pltpu.get_barrier_semaphore()
+    for partner in partners:
+        pl.semaphore_signal(barrier, inc=1, device_id=partner, device_id_type=MESH)
+
     token_copies = [
         pltpu.make_async_copy(
             tokens.at[rows_of(r)], lines[r][0].at[0], token_sem.at[r]
@@ -88,18 +94,6 @@
             part, weights.at[plane, line, which], weight_sem.at[plane, line, which]
         )
 
-    for line in range(4):
-        for plane in range(2):
-            for which in range(4):
-                weight_copy(plane, line, which).start()
-
-    partners = [at(u + 1, v), at(u - 1, v), at(u + 2, v), at(u, v + 1), at(u, v - 1)]
-    partners += [twin] + [group(d) for d in (1, 2, 3)]
-    barrier = pltpu.get_barrier_semaphore()
-    for partner in partners:
-        pl.semaphore_signal(barrier, inc=1, device_id=partner, device_id_type=MESH)
-    pl.semaphore_wait(barrier, len(partners))
-
     def half(r, way):
         return pl.ds(way * (SIZES[r] // 2), SIZES[r] // 2)
 
@@ -163,6 +157,7 @@
             far2(r, i, way).wait_recv()
         to_twin(r, 2, i).start()
 
+    pl.semaphore_wait(barrier, len(partners))
     for r in range(CHUNKS):
         open_chunk(r)
 
@@ -212,6 +207,11 @@
             state(d, k).start()
     for k in range(SLOTS):
         prior[0][k] = prior_own[(own_rows[0] >> (3 * k)) & 7].astype(BF16)
+
+    for line in range(4):
+        for plane in range(2):
+            for which in range(4):
+                weight_copy(plane, line, which).start()
 
     def multiply(part, plane, line, first, r, pair):
         left = jnp.concatenate([part[i] for i in range(4)], axis=1)

time: 60.8 us -> 59.1 us (0.972)
  Pallas kernels: 59.3 us -> 57.6 us
    pallas_call x1, Pallas kernels: 56.8 us -> 55.1 us  [on_device(): pl.pallas_call(kernel, out_shape=(jax.ShapeDtypeStruct((ROWS, HEAD), BF16...]
where the time goes in v4:
time: 59.1 us; the launch traced here: 58.9 us
  Pallas kernels  57.6 us (97%)
  between operations  1.29 us (2%)
    pallas_call x1, Pallas kernels, on_device(): pl.pallas_call(kernel, out_shape=(jax.ShapeDtypeStruct((ROWS, HEAD), BF16...  55.1 us
    pallas_call x1, Pallas kernels, on_device(): pl.pallas_call(deliver, out_shape=(jax.ShapeDtypeStruct(retained.shape, B...  2.5 us

profile of v4, /device:TPU:1, one launch (start us, length us, event | category | flops | bytes accessed | tf_op | source)
XLA Modules:
  0.0 58.9 jit_solution(7085673466657685510)
XLA Ops:
  1.3 55.1 %shard_map.113 = (bf16[512,256]{1,0:T(8,128)(2,1)}, f32[8,256,256]{2,1,0:T(8,128)}) custom-call(bf16[512,256]{1,0:T(8,128)(2,1)} %tokens.1, bf16[4,4,2,256,256]{4,3,2,1,0:T(8,128)(2,1)} %bitcast.8, bf16[4,4,2,256,256]{4,3,2,1,0:T(8,128)(2,1)} %bitcast.9, bf16[4,4,2,256,256]{4,3,2,1,0:T(8,128)(2,1)} %bitcast.10, bf16[4,4,2,256,256]{4,3,2,1,0:T(8,128)(2,1)} %bitcast.11, ...), custom_call_target="tpu_custom_call" | custom-call | flops 11000000512 | bytes 24000000 | tf_op jit(solution)/shard_map/pallas_call | solution.py:437
  56.4 2.5 %shard_map.114 = (bf16[512,256]{1,0:T(8,128)(2,1)}, f32[8,256,256]{2,1,0:T(8,128)}) custom-call(bf16[512,256]{1,0:T(8,128)(2,1)} %get-tuple-element.6.retained, f32[8,256,256]{2,1,0:T(8,128)} %get-tuple-element.7.new_states), custom_call_target="tpu_custom_call" | custom-call | tf_op jit(solution)/shard_map/pallas_call | solution.py:471

commit v5 on v4

--- a/solution.py
+++ b/solution.py
@@ -284,16 +284,15 @@
     steps = [
         (1, near_in), (2, far_in, 0), (3, near2_in), (4, far_in, 1), (5, far_in, 3), (6, far_in, 2),
         (7, far2_in, 0), (8, far2_in, 1), (9, far2_in, 3), (10, far2_in, 2),
-        (6.5, own, 0), (7.5, other, 0), (8.2, own, 1), (8.7, own, 3), (9.5, other, 1),
-        (9.7, other, 3), (10.5, own, 2), (11, other, 2), (11.5, finish),
+        (8.5, own, 0), (8.6, other, 0), (9.2, own, 1), (9.5, own, 3), (10.2, other, 1),
+        (10.3, other, 3), (10.5, own, 2), (11, other, 2), (11.5, finish),
     ]
     for r in range(CHUNKS):
         total[r][...] = jnp.zeros_like(total[r])
     order = [(when + STAGGER * r, r, *step) for r in range(CHUNKS) for when, *step in steps]
     order.append((6.4, 0, get_weights))
+    order += [(15.1 + STAGGER * r, r, pass_on) for r in range(CHUNKS - 1)]
     for _, r, step, *more in sorted(order, key=lambda entry: entry[:2]):
-        if step is finish and r > 0:
-            pass_on(r - 1)
         step(r, *more)
     rest(0)
     pass_on(CHUNKS - 1)

time: 59.1 us -> 59.1 us (level)
  no operation moved by 1% of the time
where the time goes in v5:
time: 59.1 us; the launch traced here: 58.9 us
  Pallas kernels  57.6 us (97%)
  between operations  1.29 us (2%)
    pallas_call x1, Pallas kernels, on_device(): pl.pallas_call(kernel, out_shape=(jax.ShapeDtypeStruct((ROWS, HEAD), BF16...  55.1 us
    pallas_call x1, Pallas kernels, on_device(): pl.pallas_call(deliver, out_shape=(jax.ShapeDtypeStruct(retained.shape, B...  2.5 us

profile of v5, /device:TPU:1, one launch (start us, length us, event | category | flops | bytes accessed | tf_op | source)
XLA Modules:
  0.0 58.9 jit_solution(5091154080836594136)
XLA Ops:
  1.3 55.1 %shard_map.113 = (bf16[512,256]{1,0:T(8,128)(2,1)}, f32[8,256,256]{2,1,0:T(8,128)}) custom-call(bf16[512,256]{1,0:T(8,128)(2,1)} %tokens.1, bf16[4,4,2,256,256]{4,3,2,1,0:T(8,128)(2,1)} %bitcast.8, bf16[4,4,2,256,256]{4,3,2,1,0:T(8,128)(2,1)} %bitcast.9, bf16[4,4,2,256,256]{4,3,2,1,0:T(8,128)(2,1)} %bitcast.10, bf16[4,4,2,256,256]{4,3,2,1,0:T(8,128)(2,1)} %bitcast.11, ...), custom_call_target="tpu_custom_call" | custom-call | flops 11000000512 | bytes 24000000 | tf_op jit(solution)/shard_map/pallas_call | solution.py:436
  56.4 2.5 %shard_map.114 = (bf16[512,256]{1,0:T(8,128)(2,1)}, f32[8,256,256]{2,1,0:T(8,128)}) custom-call(bf16[512,256]{1,0:T(8,128)(2,1)} %get-tuple-element.6.retained, f32[8,256,256]{2,1,0:T(8,128)} %get-tuple-element.7.new_states), custom_call_target="tpu_custom_call" | custom-call | tf_op jit(solution)/shard_map/pallas_call | solution.py:470
